TPU v7x, 32 devices: a whole 2x2x4 slice. The times are simulated.
32 devices in a mesh: seq: 16 (over z, x, core), wshard: 2 (over y).
Axes of the slice: x: 2, y: 2, z: 4, core: 2. Of those that a mesh axis runs over, the one named last changes fastest.
Arguments:
- hidden: bfloat16 [8, 2048, 1024], P('wshard', 'seq'), may hold values from -6 to 6
- segments: int32 [8, 2048], P('wshard', 'seq'), may hold values from 0 to 2, never falling along the last dimension, each value on 1 to 1536 neighbouring positions
- cotangent: bfloat16 [8, 2048, 1024], P('wshard', 'seq'), may hold values from -6 to 6
- in_weight: bfloat16 [1024, 3, 1024], P(None, None, 'wshard'), may hold values from -0.1875 to 0.1875
- out_weight: bfloat16 [1024, 1024], P('wshard'), may hold values from -0.1875 to 0.1875
- gate_weight: bfloat16 [1024, 4608], P(None, 'wshard'), may hold values from -0.1875 to 0.1875
- up_weight: bfloat16 [1024, 4608], P(None, 'wshard'), may hold values from -0.1875 to 0.1875
- down_weight: bfloat16 [4608, 1024], P('wshard'), may hold values from -0.09375 to 0.09375
- conv_weight: bfloat16 [3, 1024], P(None, 'wshard'), may hold values from -3 to 3
- norm_mix: bfloat16 [1024], P('wshard'), may hold values from 0.5 to 1.5
- norm_ffn: bfloat16 [1024], P('wshard'), may hold values from 0.5 to 1.5
Outputs:
- block_out: bfloat16 [8, 2048, 1024], P('wshard', 'seq')
- grad_hidden: float32 [8, 2048, 1024], P('wshard', 'seq')
- grad_in: float32 [1024, 3, 1024], P('seq', None, 'wshard')
- grad_out: float32 [1024, 1024], P('wshard', 'seq')
- grad_gate: float32 [1024, 4608], P('seq', 'wshard')
- grad_up: float32 [1024, 4608], P('seq', 'wshard')
- grad_down: float32 [4608, 1024], P('wshard', 'seq')
- grad_conv: float32 [3, 1024], P(None, 'wshard')
- grad_norm_mix: float32 [1024], P('wshard')
- grad_norm_ffn: float32 [1024], P('wshard')
Inputs may be any that keep to these rules, and one draw needn't show every extreme that they name: `segments`: segment numbers never fall along a sequence; each document holds 1 to 1536 tokens, one exactly that many.
All inputs are finite; a program needn't handle non-finite values.
Results may differ from a plain program's by a relative error of at most 0.017.
Values may be sent and summed in bfloat16 or wider, within the bound.
No kernel may reach another device: no remote copies, remote signals or barrier semaphores. Data moves between devices by JAX's collectives and lax.ppermute only.
A program may use at most 256 MiB of HBM per device.

v0:
```python
import jax
import jax.numpy as jnp
from jax import lax
from jax.sharding import PartitionSpec as P

EPS = 1e-05
LOW = jnp.bfloat16
F32 = jnp.float32


def over_seq(block, route):
    return lax.ppermute(block, "seq", route)


def swap_seq(block, mask):
    return over_seq(block, [(i, i ^ mask) for i in range(lax.axis_size("seq"))])


def swap_core(block):
    return swap_seq(block, 1)


def swap_pair(block):
    return lax.ppermute(block, "wshard", [(0, 1), (1, 0)])


def swap(block, link):
    return swap_pair(block) if link == "pair" else swap_seq(block, 2 * link)


def mm(left, right):
    return jnp.dot(left, right, preferred_element_type=F32)


def mm_tn(left, right):
    return lax.dot_general(left, right, (((0,), (0,)), ((), ())), preferred_element_type=F32)


def mm_nt(left, right):
    return lax.dot_general(left, right, (((1,), (1,)), ((), ())), preferred_element_type=F32)


def norm_stats(values):
    return lax.rsqrt(jnp.mean(values * values, axis=-1, keepdims=True) + EPS)


def norm_back(upstream, values, scale, gain):
    scaled = values * scale
    weighted = upstream * gain
    inner = jnp.mean(weighted * scaled, axis=-1, keepdims=True)
    return scale * (weighted - scaled * inner)


def slot_masks(order):
    masks = [0]
    for link in reversed(order):
        masks = masks + [mask ^ link for mask in masks]
    return masks


def in_slots(grad, chip, order):
    chips = lax.axis_size("seq") // 2
    blocks = grad.astype(LOW).reshape(chips, grad.shape[0] // chips, grad.shape[1])
    return jnp.stack(
        [lax.dynamic_index_in_dim(blocks, chip ^ mask, 0, False) for mask in slot_masks(order)]
    )


def halving(send, keep, order):
    terms = [keep]
    half = keep.shape[0]
    terms.append(swap(send, order[0]))
    for link in order[1:]:
        half //= 2
        going = sum((term[half : 2 * half].astype(F32) for term in terms)).astype(LOW)
        terms.append(swap(going, link))
    return sum((term[0].astype(F32) for term in terms))


def scatter_seq(grad, chip, order):
    slots = in_slots(grad, chip, order)
    half = slots.shape[0] // 2
    return halving(slots[half:], slots[:half], order)


def scatter_all(mine, other, chip, order):
    return halving(in_slots(other, chip, order[1:]), in_slots(mine, chip, order[1:]), order)


def local(
    hidden,
    segments,
    cotangent,
    in_weight,
    out_weight,
    gate_weight,
    up_weight,
    down_weight,
    conv_weight,
    norm_mix,
    norm_ffn,
):
    groups, block, width = hidden.shape
    rows = groups * block
    size = lax.axis_size("seq")
    seq_index = lax.axis_index("seq")
    core = seq_index % 2
    chip = seq_index // 2
    pair = lax.axis_index("wshard")
    first_core = core == 0
    chips = size // 2
    links = [1 << bit for bit in range(chips.bit_length() - 1)]
    features = out_weight.shape[0] // 2
    units = gate_weight.shape[1] // 2

    def ordered(flag, mine, other, axis):
        return jnp.where(
            flag,
            jnp.concatenate([mine, other], axis=axis),
            jnp.concatenate([other, mine], axis=axis),
        )

    small = jnp.concatenate([conv_weight, norm_mix[None], norm_ffn[None]], axis=0)
    small_other = swap_pair(small)
    gains = ordered(pair == 0, small[3:], small_other[3:], 1).astype(F32)
    gain_mix, gain_ffn = (gains[0], gains[1])

    def of_core(array, axis):
        return lax.dynamic_slice_in_dim(
            array, core * (array.shape[axis] // 2), array.shape[axis] // 2, axis
        )

    taps = jnp.concatenate([of_core(small[:3], 1), of_core(small_other[:3], 1)], axis=1).astype(F32)
    in_mine = of_core(jnp.transpose(in_weight, (1, 0, 2)), 2)
    in_other = swap_pair(in_mine)
    out_mine = of_core(out_weight, 0)
    out_other = swap_pair(out_mine)
    in_mat = jnp.concatenate([part for j in range(3) for part in (in_mine[j], in_other[j])], axis=1)
    out_mat = jnp.concatenate([out_mine, out_other], axis=0)
    conv_width = 2 * features
    own = hidden.reshape(rows, width)
    chip_hidden = jnp.concatenate([own, swap_core(own)], axis=0)
    seg_low = segments.astype(LOW)
    seg_other = swap_core(segments)
    edge = jnp.concatenate(
        [hidden, jnp.broadcast_to(seg_low[:, :, None], (groups, block, 128))], axis=2
    )
    last, head = (edge[:, block - 2 :], edge[:, :2])
    odd = range(1, size - 1, 2)
    even = range(2, size, 2)
    before = jnp.where(
        first_core,
        over_seq(last, [(i, i + 1) for i in odd]),
        over_seq(last, [(i, i + 2) for i in odd]),
    )
    after = jnp.where(
        first_core,
        over_seq(head, [(i, i - 2) for i in even]),
        over_seq(head, [(i, i - 1) for i in even]),
    )
    edges = jnp.concatenate([before, after], axis=0)
    edge_hidden = edges[:, :, :width].reshape(4 * groups, width)
    edge_segs = edges[:, :, width].astype(jnp.int32)
    resid = chip_hidden.astype(F32)
    scale_mix = norm_stats(resid)
    normed_mix = (resid * scale_mix * gain_mix).astype(LOW)
    edge_resid = edge_hidden.astype(F32)
    edge_normed = (edge_resid * norm_stats(edge_resid) * gain_mix).astype(LOW)
    projected = mm(normed_mix, in_mat)
    edge_projected = mm(edge_normed, in_mat)
    b_part = projected[:, :conv_width]
    c_part = projected[:, conv_width : 2 * conv_width]
    x_part = projected[:, 2 * conv_width :]

    def by_core(array):
        return array.reshape((2, groups, block) + array.shape[1:])

    def lead(own_lead, other_lead):
        return jnp.stack([own_lead, other_lead])

    conv_in = by_core((b_part * x_part).astype(LOW).astype(F32))
    edge_conv_in = (
        (edge_projected[: 2 * groups, :conv_width] * edge_projected[: 2 * groups, 2 * conv_width :])
        .astype(LOW)
        .astype(F32)
        .reshape(groups, 2, conv_width)
    )
    edge_c = edge_projected[2 * groups :, conv_width : 2 * conv_width]
    segs = jnp.stack([segments, seg_other])
    segs_before, segs_after = (edge_segs[:groups], edge_segs[groups:])

    def with_before(values, outside):
        ahead = jnp.where(
            first_core,
            lead(outside, values[0, :, block - 2 :]),
            lead(values[1, :, block - 2 :], outside),
        )
        return jnp.concatenate([ahead, values], axis=2)

    def with_after(values, outside):
        behind = jnp.where(
            first_core, lead(values[1, :, :2], outside), lead(outside, values[0, :, :2])
        )
        return jnp.concatenate([values, behind], axis=2)

    ext = with_before(conv_in, edge_conv_in)
    segs_ext = with_before(segs, segs_before)
    keep_one = (segs_ext[:, :, 1 : 1 + block] == segs).astype(F32)[..., None]
    keep_two = (segs_ext[:, :, :block] == segs).astype(F32)[..., None]
    lag_one = keep_one * ext[:, :, 1 : 1 + block]
    lag_two = keep_two * ext[:, :, :block]
    conv_out = (taps[2] * conv_in + taps[1] * lag_one + taps[0] * lag_two).reshape(
        2 * rows, conv_width
    )
    mixed = (c_part * conv_out).astype(LOW)
    mix_part = mm(mixed, out_mat).astype(LOW)
    mix_other = swap_core(mix_part)
    mix_term = mix_part.astype(F32) + jnp.concatenate(
        [mix_other[rows:], mix_other[:rows]], axis=0
    ).astype(F32)
    resid_two = resid + mix_term
    scale_ffn = norm_stats(resid_two)
    normed_ffn = (resid_two * scale_ffn * gain_ffn).astype(LOW)

    def gathered(mine):
        far = swap_pair(mine)
        return (far, swap_core(far))

    cot = cotangent.reshape(rows, width)
    cot_chip = jnp.concatenate([cot, swap_core(cot)], axis=0)
    cot_far = jnp.concatenate(gathered(cot), axis=0)
    normed_far = jnp.concatenate(gathered(normed_ffn[:rows]), axis=0)
    gate_mat = of_core(gate_weight, 1)
    up_mat = of_core(up_weight, 1)
    down_mat = of_core(down_weight, 0)

    def feed_forward(normed, upstream):
        gate = mm(normed, gate_mat)
        up_value = mm(normed, up_mat)
        d_act = mm_nt(upstream, down_mat)
        sigma = jax.nn.sigmoid(gate)
        silu_gate = gate * sigma
        act = (silu_gate * up_value).astype(LOW)
        d_gate = (d_act * up_value * sigma * (1.0 + gate * (1.0 - sigma))).astype(LOW)
        d_up = (d_act * silu_gate).astype(LOW)
        term = mm(act, down_mat).astype(LOW)
        d_normed = (mm_nt(d_gate, gate_mat) + mm_nt(d_up, up_mat)).astype(LOW)
        return (act, d_gate, d_up, term, d_normed)

    near_out = feed_forward(normed_ffn, cot_chip)
    far_out = feed_forward(normed_far, cot_far)

    def home(near, far):
        near_sum = near[:rows].astype(F32) + swap_core(near[rows:]).astype(F32)
        far_sum = (far[:rows].astype(F32) + swap_core(far[rows:]).astype(F32)).astype(LOW)
        return near_sum + swap_pair(far_sum).astype(F32)

    d_normed_ffn = home(near_out[4], far_out[4])
    block_out = (resid_two[:rows] + home(near_out[3], far_out[3])).astype(LOW)
    all_normed = jnp.concatenate([normed_ffn, normed_far], axis=0)
    all_cot = jnp.concatenate([cot_chip, cot_far], axis=0)
    act, d_gate, d_up = (jnp.concatenate([near_out[i], far_out[i]], axis=0) for i in range(3))
    part_down = scatter_seq(mm_tn(all_cot, act), chip, links)
    part_gate = scatter_seq(mm_tn(all_normed, d_gate), chip, links)
    part_up = scatter_seq(mm_tn(all_normed, d_up), chip, links)
    upstream = cot.astype(F32)
    own_two, own_scale = (resid_two[:rows], scale_ffn[:rows])
    d_resid_two = upstream + norm_back(d_normed_ffn, own_two, own_scale, gain_ffn)
    grad_gain_ffn = jnp.sum(d_normed_ffn * own_two * own_scale, axis=0)
    d_resid_low = d_resid_two.astype(LOW)
    d_chip = jnp.concatenate([d_resid_low, swap_core(d_resid_low)], axis=0)
    d_head = d_resid_low.reshape(groups, block, width)[:, :2]
    d_after = jnp.where(
        first_core,
        over_seq(d_head, [(i, i - 2) for i in even]),
        over_seq(d_head, [(i, i - 1) for i in even]),
    ).reshape(2 * groups, width)
    d_mixed = mm_nt(d_chip, out_mat)
    edge_d_conv = (mm_nt(d_after, out_mat) * edge_c).reshape(groups, 2, conv_width)
    d_conv = by_core(d_mixed * c_part)
    d_c = d_mixed * conv_out
    grad_taps = jnp.stack(
        [
            jnp.sum(d_conv * lag_two, axis=(0, 1, 2)),
            jnp.sum(d_conv * lag_one, axis=(0, 1, 2)),
            jnp.sum(d_conv * conv_in, axis=(0, 1, 2)),
        ]
    )
    d_ext = with_after(d_conv, edge_d_conv)
    segs_next = with_after(segs, segs_after)
    next_one = (segs_next[:, :, 1 : 1 + block] == segs).astype(F32)[..., None]
    next_two = (segs_next[:, :, 2 : 2 + block] == segs).astype(F32)[..., None]
    d_conv_in = (
        taps[2] * d_conv
        + taps[1] * next_one * d_ext[:, :, 1 : 1 + block]
        + taps[0] * next_two * d_ext[:, :, 2 : 2 + block]
    ).reshape(2 * rows, conv_width)
    d_proj = jnp.concatenate([d_conv_in * x_part, d_c, d_conv_in * b_part], axis=1).astype(LOW)
    grad_out = mm_tn(d_chip, mixed)
    grad_in = mm_tn(normed_mix, d_proj)
    d_normed_part = mm_nt(d_proj, in_mat).astype(LOW)
    d_normed_mix = d_normed_part[:rows].astype(F32) + swap_core(d_normed_part[rows:]).astype(F32)
    own_resid, own_mix = (resid[:rows], scale_mix[:rows])
    grad_hidden = (d_resid_two + norm_back(d_normed_mix, own_resid, own_mix, gain_mix)).reshape(
        groups, block, width
    )
    grad_gain_mix = jnp.sum(d_normed_mix * own_resid * own_mix, axis=0)
    halves = [grad_out] + [grad_in[:, j * conv_width : (j + 1) * conv_width] for j in range(3)]
    mixed_mine = jnp.concatenate([half[:, :features] for half in halves], axis=1)
    mixed_far = jnp.concatenate([half[:, features:] for half in halves], axis=1)
    part_mix = scatter_all(mixed_mine, mixed_far, chip, ["pair"] + links)
    part_rows = width // size

    def finish(part):
        low = part.astype(LOW).reshape(2, part_rows, -1)
        came = swap_core(lax.dynamic_index_in_dim(low, 1 - core, 0, False)).astype(F32)
        mine = lax.dynamic_index_in_dim(part.reshape(2, part_rows, -1), core, 0, False)
        return (mine, came)

    def wide(part):
        mine, came = finish(part)
        return ordered(first_core, mine, came, 1)

    out_down = wide(part_down).T
    out_gate = wide(part_gate)
    out_up = wide(part_up)
    mix_mine, mix_came = finish(part_mix)
    mix_parts = [
        ordered(
            first_core,
            mix_mine[:, j * features : (j + 1) * features],
            mix_came[:, j * features : (j + 1) * features],
            1,
        )
        for j in range(4)
    ]
    out_out = mix_parts[0].T
    out_in = jnp.stack(mix_parts[1:], axis=1)
    half_width = norm_mix.shape[0]
    spread = jnp.zeros((3, width), F32)
    spread = lax.dynamic_update_slice_in_dim(
        spread, grad_taps[:, :features], pair * half_width + core * features, 1
    )
    spread = lax.dynamic_update_slice_in_dim(
        spread, grad_taps[:, features:], (1 - pair) * half_width + core * features, 1
    )
    sums = lax.psum(
        jnp.concatenate([spread, grad_gain_mix[None], grad_gain_ffn[None]], axis=0),
        ("seq", "wshard"),
    )
    sums = lax.dynamic_slice_in_dim(sums, pair * half_width, half_width, 1)
    return (
        block_out.reshape(groups, block, width),
        grad_hidden,
        out_in,
        out_out,
        out_gate,
        out_up,
        out_down,
        sums[:3],
        sums[3],
        sums[4],
    )


def solution(mesh):
    return jax.shard_map(
        local,
        mesh=mesh,
        in_specs=(
            P("wshard", "seq", None),
            P("wshard", "seq"),
            P("wshard", "seq", None),
            P(None, None, "wshard"),
            P("wshard", None),
            P(None, "wshard"),
            P(None, "wshard"),
            P("wshard", None),
            P(None, "wshard"),
            P("wshard"),
            P("wshard"),
        ),
        out_specs=(
            P("wshard", "seq", None),
            P("wshard", "seq", None),
            P("seq", None, "wshard"),
            P("wshard", "seq"),
            P("seq", "wshard"),
            P("seq", "wshard"),
            P("wshard", "seq"),
            P(None, "wshard"),
            P("wshard"),
            P("wshard"),
        ),
        check_vma=False,
    )
```

profile of v0, /device:TPU:0, one launch (start us, length us, event | category | flops | bytes accessed | tf_op | source)
XLA Modules:
  0.0 517.6 jit_solution(11000948463357092600)
XLA Ops:
  0.7 3.2 copy.56
  9.0 3.0 collective-permute-start.2
  12.7 4.7 collective-permute-start.7
  21.6 25.2 %collective-permute-done.1 = bf16[5,512]{1,0:T(8,128)(2,1)S(1)} collective-permute-done((bf16[5,512]{1,0:T(8,128)(2,1)S(1)}, bf16[5,512]{1,0:T(8,128)(2,1)S(1)}, u32[]{:S(2)}, u32[]{:S(2)}) %collective-permute-start.1) | collective-permute-done | bytes 5152 | tf_op jit(solution)/shard_map/ppermute | solution.py:24
  52.9 2.0 fusion.78
  54.8 2.0 fusion.77
  58.7 1.9 fusion.75
  60.6 2.4 fusion.86
  63.7 5.4 %fusion.73 = f32[1024,1536]{1,0:T(8,128)S(1)} fusion(bf16[1024,1536]{1,0:T(8,128)(2,1)} %fusion.75, f32[1024]{0:T(1024)S(1)} %bitcast.190, f32[1024]{0:T(1024)S(1)} %add_rsqrt_fusion.1, bf16[512,1024]{1,0:T(8,128)(2,1)S(1)} %collective-permute-done, bf16[512,1024]{1,0:T(8,128)(2,1)S(1)} %bitcast.148), kind=kOutput, calls=%fused_computation.131 | convolution fusion | flops 3228565504 | bytes 11542528 | tf_op jit(solution)/shard_map/dot_general | solution.py:32
  73.1 4.2 convolution_convert_fusion.4
  79.7 23.4 %collective-permute-done.17 = bf16[512,1024]{1,0:T(8,128)(2,1)} collective-permute-done((bf16[512,1024]{1,0:T(8,128)(2,1)}, bf16[512,1024]{1,0:T(8,128)(2,1)}, u32[]{:S(2)}, u32[]{:S(2)}) %collective-permute-start.17) | collective-permute-done | bytes 1048608 | tf_op jit(solution)/shard_map/ppermute | solution.py:24
  103.1 3.6 fusion.121
  108.7 2.7 multiply_reduce_fusion
  113.5 4.5 fusion.61
  118.0 4.5 fusion.69
  122.6 9.7 %multiply_convert_fusion.2 = (bf16[1024,1152]{1,0:T(8,128)(2,1)S(1)}, bf16[1024,1152]{1,0:T(8,128)(2,1)}, bf16[1024,1152]{1,0:T(8,128)(2,1)}) fusion(f32[1024,1152]{1,0:T(8,128)} %fusion.69, f32[1024,1152]{1,0:T(8,128)} %fusion.61, bf16[2304,1024]{1,0:T(8,128)(2,1)S(1)} %bitcast.220, s32[]{:T(128)S(6)} %select_n.227, ...), kind=kOutput, calls=%fused_computation.14 | convolution fusion | flops 2437808128 | bytes 20971524 | tf_op jit(solution)/shard_map/dot_general | solution.py:40
  132.3 6.1 %fusion.65 = f32[1024,1024]{1,0:T(8,128)S(1)} fusion(bf16[1024,1152]{1,0:T(8,128)(2,1)} %get-tuple-element.24, bf16[1024,2304]{1,0:T(8,128)(2,1)} %param.16, s32[]{:T(128)S(6)} %select_n.227), kind=kOutput, calls=%fused_computation.113 | convolution fusion | flops 2415919104 | bytes 8912900 | tf_op jit(solution)/shard_map/dot_general | solution.py:40
  138.8 5.0 add_convert_fusion.1
  145.1 3.3 convolution_convert_fusion.2
  149.6 4.5 fusion.59
  154.1 4.5 fusion.67
  158.6 11.4 %multiply_convert_fusion = (bf16[1024,1152]{1,0:T(8,128)(2,1)S(1)}, bf16[1024,1152]{1,0:T(8,128)(2,1)}, bf16[1024,1152]{1,0:T(8,128)(2,1)}) fusion(f32[1024,1152]{1,0:T(8,128)} %fusion.67, f32[1024,1152]{1,0:T(8,128)} %fusion.59, bf16[2304,1024]{1,0:T(8,128)(2,1)} %param.18, s32[]{:T(128)S(6)} %select_n.227, bf16[512,1024]{1,0:T(8,128)(2,1)} %collective-permute-done.18, ...), kind=kOutput, calls=%fused_computation.12 | convolution fusion | flops 2437808128 | bytes 20971524 | tf_op jit(solution)/shard_map/dot_general | solution.py:40
  170.1 6.1 %convolution_convert_fusion.1 = bf16[1024,1024]{1,0:T(8,128)(2,1)S(1)} fusion(bf16[1024,1152]{1,0:T(8,128)(2,1)} %get-tuple-element.28, bf16[2304,1024]{1,0:T(8,128)(2,1)} %param.18, s32[]{:T(128)S(6)} %select_n.227), kind=kOutput, calls=%fused_computation.96 | convolution fusion | flops 2416967680 | bytes 6815748 | tf_op jit(solution)/shard_map/dot_general | solution.py:32
  177.6 4.6 fusion.63
  182.2 3.6 add_convert_fusion
  187.7 9.3 %fusion.21 = bf16[1024,1152]{1,0:T(8,128)(2,1)S(1)} fusion(bf16[1024,1152]{1,0:T(8,128)(2,1)} %get-tuple-element.28, bf16[1024,1152]{1,0:T(8,128)(2,1)} %get-tuple-element.25, bf16[512,1024]{1,0:T(8,128)(2,1)} %collective-permute-done.18, bf16[512,1024]{1,0:T(8,128)(2,1)} %collective-permute-done.17, bf16[512,1024]{1,0:T(8,128)(2,1)} %collective-permute-done.15, ...), kind=kOutput, calls=%fused_computation.37 | convolution fusion | flops 4859232256 | bytes 11272192 | tf_op jit(solution)/shard_map/dot_general | solution.py:36
  199.9 8.2 %fusion.26 = bf16[1024,1152]{1,0:T(8,128)(2,1)S(1)} fusion(bf16[1024,1152]{1,0:T(8,128)(2,1)} %copy-done.38, bf16[1024,1152]{1,0:T(8,128)(2,1)} %copy-done.37, bf16[512,1024]{1,0:T(8,128)(2,1)S(1)} %collective-permute-done.12, bf16[512,1024]{1,0:T(8,128)(2,1)S(1)} %collective-permute-done.11, bf16[1024,1024]{1,0:T(8,128)(2,1)S(1)} %multiply_convert_fusion.6), kind=kOutput, calls=%fused_computation.38 | convolution fusion | flops 4855037952 | bytes 11272192 | tf_op jit(solution)/shard_map/dot_general | solution.py:36
  210.2 8.8 %fusion.29 = bf16[1024,1152]{1,0:T(8,128)(2,1)S(1)} fusion(bf16[1024,1152]{1,0:T(8,128)(2,1)} %get-tuple-element.27, bf16[1024,1152]{1,0:T(8,128)(2,1)} %get-tuple-element.24, bf16[512,1024]{1,0:T(8,128)(2,1)} %copy-done.24, bf16[512,1024]{1,0:T(8,128)(2,1)} %copy-done.23, bf16[1024,1024]{1,0:T(8,128)(2,1)S(1)} %multiply_convert_fusion.6), kind=kOutput, calls=%fused_computation.39 | convolution fusion | flops 4855037952 | bytes 11272192 | tf_op jit(solution)/shard_map/dot_general | solution.py:36
  229.3 23.5 %collective-permute-done.34 = bf16[4,128,1152]{2,1,0:T(8,128)(2,1)} collective-permute-done((bf16[4,128,1152]{2,1,0:T(8,128)(2,1)}, bf16[4,128,1152]{2,1,0:T(8,128)(2,1)}, u32[]{:S(2)}, u32[]{:S(2)}) %collective-permute-start.34) | collective-permute-done | bytes 1179680 | tf_op jit(solution)/shard_map/ppermute | solution.py:12
  255.6 21.7 %collective-permute-done.30 = bf16[4,128,1152]{2,1,0:T(8,128)(2,1)S(1)} collective-permute-done((bf16[4,128,1152]{2,1,0:T(8,128)(2,1)S(1)}, bf16[4,128,1152]{2,1,0:T(8,128)(2,1)S(1)}, u32[]{:S(2)}, u32[]{:S(2)}) %collective-permute-start.30) | collective-permute-done | bytes 1179680 | tf_op jit(solution)/shard_map/ppermute | solution.py:12
  280.6 12.9 %collective-permute-done.35 = bf16[2,128,1152]{2,1,0:T(8,128)(2,1)S(1)} collective-permute-done((bf16[2,128,1152]{2,1,0:T(8,128)(2,1)S(1)}, bf16[2,128,1152]{2,1,0:T(8,128)(2,1)S(1)}, u32[]{:S(2)}, u32[]{:S(2)}) %collective-permute-start.35) | collective-permute-done | bytes 589856 | tf_op jit(solution)/shard_map/ppermute | solution.py:12
  295.3 9.3 %collective-permute-done.31 = bf16[2,128,1152]{2,1,0:T(8,128)(2,1)S(1)} collective-permute-done((bf16[2,128,1152]{2,1,0:T(8,128)(2,1)S(1)}, bf16[2,128,1152]{2,1,0:T(8,128)(2,1)S(1)}, u32[]{:S(2)}, u32[]{:S(2)}) %collective-permute-start.31) | collective-permute-done | bytes 589856 | tf_op jit(solution)/shard_map/ppermute | solution.py:12
  304.6 2.6 collective-permute-start.40
  307.3 11.9 %collective-permute-done.40 = bf16[1,128,1152]{2,1,0:T(8,128)(2,1)S(1)} collective-permute-done((bf16[1,128,1152]{2,1,0:T(8,128)(2,1)S(1)}, bf16[1,128,1152]{2,1,0:T(8,128)(2,1)S(1)}, u32[]{:S(2)}, u32[]{:S(2)}) %collective-permute-start.40) | collective-permute-done | bytes 294944 | tf_op jit(solution)/shard_map/ppermute | solution.py:12
  320.3 14.0 %collective-permute-done.36 = bf16[1,128,1152]{2,1,0:T(8,128)(2,1)S(1)} collective-permute-done((bf16[1,128,1152]{2,1,0:T(8,128)(2,1)S(1)}, bf16[1,128,1152]{2,1,0:T(8,128)(2,1)S(1)}, u32[]{:S(2)}, u32[]{:S(2)}) %collective-permute-start.36) | collective-permute-done | bytes 294944 | tf_op jit(solution)/shard_map/ppermute | solution.py:12
  336.9 11.6 %collective-permute-done.32 = bf16[1,128,1152]{2,1,0:T(8,128)(2,1)S(1)} collective-permute-done((bf16[1,128,1152]{2,1,0:T(8,128)(2,1)S(1)}, bf16[1,128,1152]{2,1,0:T(8,128)(2,1)S(1)}, u32[]{:S(2)}, u32[]{:S(2)}) %collective-permute-start.32) | collective-permute-done | bytes 294944 | tf_op jit(solution)/shard_map/ppermute | solution.py:12
  349.6 4.0 fusion.122
  359.1 2.5 collective-permute-done.22
  366.2 4.6 multiply_reduce_fusion.6
  374.0 2.9 convolution_convert_fusion.5
  377.0 3.7 convolution_convert_fusion
  384.8 3.7 convolution_convert_fusion.3
  389.9 40.0 %collective-permute-done.25 = bf16[8,128,1024]{2,1,0:T(8,128)(2,1)S(1)} collective-permute-done((bf16[8,128,1024]{2,1,0:T(8,128)(2,1)S(1)}, bf16[8,128,1024]{2,1,0:T(8,128)(2,1)S(1)}, u32[]{:S(2)}, u32[]{:S(2)}) %collective-permute-start.25) | collective-permute-done | bytes 2097184 | tf_op jit(solution)/shard_map/ppermute | solution.py:24
  430.3 3.0 collective-permute-start.26
  435.1 21.7 %collective-permute-done.26 = bf16[4,128,1024]{2,1,0:T(8,128)(2,1)S(1)} collective-permute-done((bf16[4,128,1024]{2,1,0:T(8,128)(2,1)S(1)}, bf16[4,128,1024]{2,1,0:T(8,128)(2,1)S(1)}, u32[]{:S(2)}, u32[]{:S(2)}) %collective-permute-start.26) | collective-permute-done | bytes 1048608 | tf_op jit(solution)/shard_map/ppermute | solution.py:12
  457.3 2.0 multiply_add_fusion
  459.2 11.3 %collective-permute-done.27 = bf16[2,128,1024]{2,1,0:T(8,128)(2,1)S(1)} collective-permute-done((bf16[2,128,1024]{2,1,0:T(8,128)(2,1)S(1)}, bf16[2,128,1024]{2,1,0:T(8,128)(2,1)S(1)}, u32[]{:S(2)}, u32[]{:S(2)}) %collective-permute-start.27) | collective-permute-done | bytes 524320 | tf_op jit(solution)/shard_map/ppermute | solution.py:12
  471.4 40.1 %psum.7 = f32[5,1024]{1,0:T(8,128)S(1)} all-reduce(f32[5,1024]{1,0:T(8,128)S(1)} %pad_maximum_fusion.23), channel_id=1, replica_groups=mesh['seq'=16,'wshard'=2] {'seq','wshard'}, use_global_device_ids=true, to_apply=%region_10.11 | all-reduce | flops 5120 | bytes 40960 | tf_op jit(solution)/shard_map/psum | solution.py:347
  (326 shorter events, 90.9 us)
Async XLA Ops:
  5.7 41.8 %collective-permute-start.5 = (bf16[4,2,1152]{2,0,1:T(4,128)(2,1)S(1)}, bf16[4,2,1152]{2,0,1:T(4,128)(2,1)S(1)}, u32[]{:S(2)}, u32[]{:S(2)}) collective-permute-start(bf16[4,2,1152]{2,0,1:T(4,128)(2,1)S(1)} %get-tuple-element.69), channel_id=1, source_target_pairs={{4,0},{8,4},{12,8},{16,12},{20,16},{24,20},{28,24},{5,1},{9,5},{13... | collective-permute-start | bytes 55304 | tf_op jit(solution)/shard_map/ppermute | solution.py:12
  7.0 41.0 %collective-permute-start.6 = (bf16[4,2,1152]{2,0,1:T(4,128)(2,1)S(1)}, bf16[4,2,1152]{2,0,1:T(4,128)(2,1)S(1)}, u32[]{:S(2)}, u32[]{:S(2)}) collective-permute-start(bf16[4,2,1152]{2,0,1:T(4,128)(2,1)S(1)} %get-tuple-element.69), channel_id=1, source_target_pairs={{4,2},{8,6},{12,10},{16,14},{20,18},{24,22},{28,26},{5,3},{9,7},{1... | collective-permute-start | bytes 55304 | tf_op jit(solution)/shard_map/ppermute | solution.py:12
  9.0 38.6 %copy-start.6 = (bf16[4,128,1024]{2,1,0:T(8,128)(2,1)S(1)}, bf16[4,128,1024]{2,1,0:T(8,128)(2,1)}, u32[]{:S(2)}) copy-start(bf16[4,128,1024]{2,1,0:T(8,128)(2,1)} %param.11) | copy-start | bytes 3145732
  9.0 42.0 %collective-permute-start.2 = (bf16[3,1024,256]{2,1,0:T(8,128)(2,1)}, bf16[3,1024,256]{2,1,0:T(8,128)(2,1)}, u32[]{:S(2)}, u32[]{:S(2)}) collective-permute-start(bf16[3,1024,256]{2,1,0:T(8,128)(2,1)} %dynamic-slice_bitcast_fusion), channel_id=1, source_target_pairs={{0,1},{1,0},{2,3},{3,2},{4,5},{5,4},{6,7},{7,6},{8,9},{9,8},{10,11... | collective-permute-start | bytes 4718600 | tf_op jit(solution)/shard_map/ppermute | solution.py:24
  11.9 37.5 %collective-permute-start.3 = (bf16[4,2,1152]{2,0,1:T(4,128)(2,1)S(1)}, bf16[4,2,1152]{2,0,1:T(4,128)(2,1)S(1)}, u32[]{:S(2)}, u32[]{:S(2)}) collective-permute-start(bf16[4,2,1152]{2,0,1:T(4,128)(2,1)S(1)} %get-tuple-element.68), channel_id=1, source_target_pairs={{2,4},{6,8},{10,12},{14,16},{18,20},{22,24},{26,28},{3,5},{7,9},{1... | collective-permute-start | bytes 55304 | tf_op jit(solution)/shard_map/ppermute | solution.py:12
  12.7 8.6 %collective-permute-start.7 = (s32[4,128]{0,1:T(8,128)S(1)}, s32[4,128]{0,1:T(8,128)S(1)}, u32[]{:S(2)}, u32[]{:S(2)}) collective-permute-start(s32[4,128]{0,1:T(8,128)S(1)} %copy.57), channel_id=1, source_target_pairs={{0,2},{2,0},{4,6},{6,4},{8,10},{10,8},{12,14},{14,12},{16,18},{18,... | collective-permute-start | bytes 6152 | tf_op jit(solution)/shard_map/ppermute | solution.py:12
  21.3 25.4 %collective-permute-start.1 = (bf16[5,512]{1,0:T(8,128)(2,1)S(1)}, bf16[5,512]{1,0:T(8,128)(2,1)S(1)}, u32[]{:S(2)}, u32[]{:S(2)}) collective-permute-start(bf16[5,512]{1,0:T(8,128)(2,1)S(1)} %pad_maximum_fusion.26), channel_id=1, source_target_pairs={{0,1},{1,0},{2,3},{3,2},{4,5},{5,4},{6,7},{7,6},{8,9},{9,8},{10,11... | collective-permute-start | bytes 15368 | tf_op jit(solution)/shard_map/ppermute | solution.py:24
  46.7 2.7 collective-permute-start.4
  47.5 2.9 collective-permute-start
  48.0 25.1 %collective-permute-start.8 = (bf16[256,1024]{1,0:T(8,128)(2,1)}, bf16[256,1024]{1,0:T(8,128)(2,1)}, u32[]{:S(2)}, u32[]{:S(2)}) collective-permute-start(bf16[256,1024]{1,0:T(8,128)(2,1)} %constant_dynamic-slice_fusion.25), channel_id=1, source_target_pairs={{0,1},{1,0},{2,3},{3,2},{4,5},{5,4},{6,7},{7,6},{8,9},{9,8},{10,11... | collective-permute-start | bytes 1572872 | tf_op jit(solution)/shard_map/ppermute | solution.py:24
  50.9 28.2 %copy-start.31 = (f32[1024]{0:T(1024)}, f32[1024]{0:T(1024)S(1)}, u32[]{:S(2)}) copy-start(f32[1024]{0:T(1024)S(1)} %add_rsqrt_fusion.1) | copy-start | bytes 12292
  77.2 29.5 %collective-permute-start.9 = (bf16[1024,1024]{1,0:T(8,128)(2,1)}, bf16[1024,1024]{1,0:T(8,128)(2,1)}, u32[]{:S(2)}, u32[]{:S(2)}) collective-permute-start(bf16[1024,1024]{1,0:T(8,128)(2,1)} %convolution_convert_fusion.4), channel_id=1, source_target_pairs={{0,2},{2,0},{4,6},{6,4},{8,10},{10,8},{12,14},{14,12},{16,18},{18,... | collective-permute-start | bytes 6291464 | tf_op jit(solution)/shard_map/ppermute | solution.py:12
  77.5 25.7 %collective-permute-start.17 = (bf16[512,1024]{1,0:T(8,128)(2,1)}, bf16[512,1024]{1,0:T(8,128)(2,1)}, u32[]{:S(2)}, u32[]{:S(2)}) collective-permute-start(bf16[512,1024]{1,0:T(8,128)(2,1)} %bitcast.18), channel_id=1, source_target_pairs={{0,1},{1,0},{2,3},{3,2},{4,5},{5,4},{6,7},{7,6},{8,9},{9,8},{10,11... | collective-permute-start | bytes 3145736 | tf_op jit(solution)/shard_map/ppermute | solution.py:24
  78.9 43.6 %collective-permute-start.15 = (bf16[512,1024]{1,0:T(8,128)(2,1)}, bf16[512,1024]{1,0:T(8,128)(2,1)}, u32[]{:S(2)}, u32[]{:S(2)}) collective-permute-start(bf16[512,1024]{1,0:T(8,128)(2,1)} %bitcast.18), channel_id=1, source_target_pairs={{0,2},{2,0},{4,6},{6,4},{8,10},{10,8},{12,14},{14,12},{16,18},{18,... | collective-permute-start | bytes 3145736 | tf_op jit(solution)/shard_map/ppermute | solution.py:12
  103.1 55.5 %collective-permute-start.18 = (bf16[512,1024]{1,0:T(8,128)(2,1)}, bf16[512,1024]{1,0:T(8,128)(2,1)}, u32[]{:S(2)}, u32[]{:S(2)}) collective-permute-start(bf16[512,1024]{1,0:T(8,128)(2,1)} %collective-permute-done.17), channel_id=1, source_target_pairs={{0,2},{2,0},{4,6},{6,4},{8,10},{10,8},{12,14},{14,12},{16,18},{18,... | collective-permute-start | bytes 3145736 | tf_op jit(solution)/shard_map/ppermute | solution.py:12
  111.9 26.5 %collective-permute-start.11 = (bf16[512,1024]{1,0:T(8,128)(2,1)S(1)}, bf16[512,1024]{1,0:T(8,128)(2,1)S(1)}, u32[]{:S(2)}, u32[]{:S(2)}) collective-permute-start(bf16[512,1024]{1,0:T(8,128)(2,1)S(1)} %slice.503), channel_id=1, source_target_pairs={{0,1},{1,0},{2,3},{3,2},{4,5},{5,4},{6,7},{7,6},{8,9},{9,8},{10,11... | collective-permute-start | bytes 3145736 | tf_op jit(solution)/shard_map/ppermute | solution.py:24
  138.4 61.4 %copy-start.23 = (bf16[512,1024]{1,0:T(8,128)(2,1)}, bf16[512,1024]{1,0:T(8,128)(2,1)S(1)}, u32[]{:S(2)}) copy-start(bf16[512,1024]{1,0:T(8,128)(2,1)S(1)} %collective-permute-done.11) | copy-start | bytes 3145732
  138.4 11.1 %collective-permute-start.12 = (bf16[512,1024]{1,0:T(8,128)(2,1)S(1)}, bf16[512,1024]{1,0:T(8,128)(2,1)S(1)}, u32[]{:S(2)}, u32[]{:S(2)}) collective-permute-start(bf16[512,1024]{1,0:T(8,128)(2,1)S(1)} %collective-permute-done.11), channel_id=1, source_target_pairs={{0,2},{2,0},{4,6},{6,4},{8,10},{10,8},{12,14},{14,12},{16,18},{18,... | collective-permute-start | bytes 3145736 | tf_op jit(solution)/shard_map/ppermute | solution.py:12
  144.8 203.8 %collective-permute-start.16 = (bf16[512,1024]{1,0:T(8,128)(2,1)}, bf16[512,1024]{1,0:T(8,128)(2,1)S(1)}, u32[]{:S(2)}, u32[]{:S(2)}) collective-permute-start(bf16[512,1024]{1,0:T(8,128)(2,1)} %slice.507), channel_id=1, source_target_pairs={{0,2},{2,0},{4,6},{6,4},{8,10},{10,8},{12,14},{14,12},{16,18},{18,... | collective-permute-start | bytes 3145736 | tf_op jit(solution)/shard_map/ppermute | solution.py:12
  149.5 50.4 %copy-start.24 = (bf16[512,1024]{1,0:T(8,128)(2,1)}, bf16[512,1024]{1,0:T(8,128)(2,1)S(1)}, u32[]{:S(2)}) copy-start(bf16[512,1024]{1,0:T(8,128)(2,1)S(1)} %collective-permute-done.12) | copy-start | bytes 3145732
  177.3 42.1 %collective-permute-start.13 = (bf16[512,1024]{1,0:T(8,128)(2,1)}, bf16[512,1024]{1,0:T(8,128)(2,1)}, u32[]{:S(2)}, u32[]{:S(2)}) collective-permute-start(bf16[512,1024]{1,0:T(8,128)(2,1)} %slice.505), channel_id=1, source_target_pairs={{0,2},{2,0},{4,6},{6,4},{8,10},{10,8},{12,14},{14,12},{16,18},{18,... | collective-permute-start | bytes 3145736 | tf_op jit(solution)/shard_map/ppermute | solution.py:12
  187.4 35.1 %collective-permute-start.19 = (bf16[512,1024]{1,0:T(8,128)(2,1)}, bf16[512,1024]{1,0:T(8,128)(2,1)}, u32[]{:S(2)}, u32[]{:S(2)}) collective-permute-start(bf16[512,1024]{1,0:T(8,128)(2,1)} %slice.509), channel_id=1, source_target_pairs={{0,2},{2,0},{4,6},{6,4},{8,10},{10,8},{12,14},{14,12},{16,18},{18,... | collective-permute-start | bytes 3145736 | tf_op jit(solution)/shard_map/ppermute | solution.py:12
  198.4 29.1 %collective-permute-start.38 = (bf16[4,128,1152]{2,1,0:T(8,128)(2,1)}, bf16[4,128,1152]{2,1,0:T(8,128)(2,1)}, u32[]{:S(2)}, u32[]{:S(2)}) collective-permute-start(bf16[4,128,1152]{2,1,0:T(8,128)(2,1)} %pad_maximum_fusion.16), channel_id=1, source_target_pairs={{0,4},{2,6},{4,0},{6,2},{8,12},{10,14},{12,8},{14,10},{16,20},{18,... | collective-permute-start | bytes 3538952 | tf_op jit(solution)/shard_map/ppermute | solution.py:12
  209.7 43.1 %collective-permute-start.34 = (bf16[4,128,1152]{2,1,0:T(8,128)(2,1)}, bf16[4,128,1152]{2,1,0:T(8,128)(2,1)}, u32[]{:S(2)}, u32[]{:S(2)}) collective-permute-start(bf16[4,128,1152]{2,1,0:T(8,128)(2,1)} %pad_maximum_fusion.15), channel_id=1, source_target_pairs={{0,4},{2,6},{4,0},{6,2},{8,12},{10,14},{12,8},{14,10},{16,20},{18,... | collective-permute-start | bytes 3538952 | tf_op jit(solution)/shard_map/ppermute | solution.py:12
  220.2 129.4 %collective-permute-start.10 = (bf16[512,1024]{1,0:T(8,128)(2,1)S(1)}, bf16[512,1024]{1,0:T(8,128)(2,1)S(1)}, u32[]{:S(2)}, u32[]{:S(2)}) collective-permute-start(bf16[512,1024]{1,0:T(8,128)(2,1)S(1)} %copy-done.22), channel_id=1, source_target_pairs={{0,2},{2,0},{4,6},{6,4},{8,10},{10,8},{12,14},{14,12},{16,18},{18,... | collective-permute-start | bytes 3145736 | tf_op jit(solution)/shard_map/ppermute | solution.py:12
  222.5 54.8 %collective-permute-start.30 = (bf16[4,128,1152]{2,1,0:T(8,128)(2,1)S(1)}, bf16[4,128,1152]{2,1,0:T(8,128)(2,1)S(1)}, u32[]{:S(2)}, u32[]{:S(2)}) collective-permute-start(bf16[4,128,1152]{2,1,0:T(8,128)(2,1)S(1)} %pad_maximum_fusion.14), channel_id=1, source_target_pairs={{0,4},{2,6},{4,0},{6,2},{8,12},{10,14},{12,8},{14,10},{16,20},{18,... | collective-permute-start | bytes 3538952 | tf_op jit(solution)/shard_map/ppermute | solution.py:12
  227.5 122.1 %collective-permute-start.14 = (bf16[512,1024]{1,0:T(8,128)(2,1)S(1)}, bf16[512,1024]{1,0:T(8,128)(2,1)S(1)}, u32[]{:S(2)}, u32[]{:S(2)}) collective-permute-start(bf16[512,1024]{1,0:T(8,128)(2,1)S(1)} %add_convert_fusion.5), channel_id=1, source_target_pairs={{0,1},{1,0},{2,3},{3,2},{4,5},{5,4},{6,7},{7,6},{8,9},{9,8},{10,11... | collective-permute-start | bytes 3145736 | tf_op jit(solution)/shard_map/ppermute | solution.py:24
  252.8 26.2 %collective-permute-start.39 = (bf16[2,128,1152]{2,1,0:T(8,128)(2,1)S(1)}, bf16[2,128,1152]{2,1,0:T(8,128)(2,1)S(1)}, u32[]{:S(2)}, u32[]{:S(2)}) collective-permute-start(bf16[2,128,1152]{2,1,0:T(8,128)(2,1)S(1)} %add_convert_fusion.6), channel_id=1, source_target_pairs={{0,8},{2,10},{4,12},{6,14},{8,0},{10,2},{12,4},{14,6},{16,24},{18,... | collective-permute-start | bytes 1769480 | tf_op jit(solution)/shard_map/ppermute | solution.py:12
  277.3 16.3 %collective-permute-start.35 = (bf16[2,128,1152]{2,1,0:T(8,128)(2,1)S(1)}, bf16[2,128,1152]{2,1,0:T(8,128)(2,1)S(1)}, u32[]{:S(2)}, u32[]{:S(2)}) collective-permute-start(bf16[2,128,1152]{2,1,0:T(8,128)(2,1)S(1)} %add_convert_fusion.7), channel_id=1, source_target_pairs={{0,8},{2,10},{4,12},{6,14},{8,0},{10,2},{12,4},{14,6},{16,24},{18,... | collective-permute-start | bytes 1769480 | tf_op jit(solution)/shard_map/ppermute | solution.py:12
  279.0 25.6 %collective-permute-start.31 = (bf16[2,128,1152]{2,1,0:T(8,128)(2,1)S(1)}, bf16[2,128,1152]{2,1,0:T(8,128)(2,1)S(1)}, u32[]{:S(2)}, u32[]{:S(2)}) collective-permute-start(bf16[2,128,1152]{2,1,0:T(8,128)(2,1)S(1)} %add_convert_fusion.8), channel_id=1, source_target_pairs={{0,8},{2,10},{4,12},{6,14},{8,0},{10,2},{12,4},{14,6},{16,24},{18,... | collective-permute-start | bytes 1769480 | tf_op jit(solution)/shard_map/ppermute | solution.py:12
  293.6 55.1 %collective-permute-start.20 = (bf16[512,1024]{1,0:T(8,128)(2,1)S(1)}, bf16[512,1024]{1,0:T(8,128)(2,1)S(1)}, u32[]{:S(2)}, u32[]{:S(2)}) collective-permute-start(bf16[512,1024]{1,0:T(8,128)(2,1)S(1)} %add_convert_fusion.3), channel_id=1, source_target_pairs={{0,1},{1,0},{2,3},{3,2},{4,5},{5,4},{6,7},{7,6},{8,9},{9,8},{10,11... | collective-permute-start | bytes 3145736 | tf_op jit(solution)/shard_map/ppermute | solution.py:24
  304.6 14.6 %collective-permute-start.40 = (bf16[1,128,1152]{2,1,0:T(8,128)(2,1)S(1)}, bf16[1,128,1152]{2,1,0:T(8,128)(2,1)S(1)}, u32[]{:S(2)}, u32[]{:S(2)}) collective-permute-start(bf16[1,128,1152]{2,1,0:T(8,128)(2,1)S(1)} %add_convert_fusion.10), channel_id=1, source_target_pairs={{0,16},{2,18},{4,20},{6,22},{8,24},{10,26},{12,28},{14,30},{16,0},... | collective-permute-start | bytes 884744 | tf_op jit(solution)/shard_map/ppermute | solution.py:12
  319.2 15.1 %collective-permute-start.36 = (bf16[1,128,1152]{2,1,0:T(8,128)(2,1)S(1)}, bf16[1,128,1152]{2,1,0:T(8,128)(2,1)S(1)}, u32[]{:S(2)}, u32[]{:S(2)}) collective-permute-start(bf16[1,128,1152]{2,1,0:T(8,128)(2,1)S(1)} %add_convert_fusion.11), channel_id=1, source_target_pairs={{0,16},{2,18},{4,20},{6,22},{8,24},{10,26},{12,28},{14,30},{16,0},... | collective-permute-start | bytes 884744 | tf_op jit(solution)/shard_map/ppermute | solution.py:12
  334.3 14.2 %collective-permute-start.32 = (bf16[1,128,1152]{2,1,0:T(8,128)(2,1)S(1)}, bf16[1,128,1152]{2,1,0:T(8,128)(2,1)S(1)}, u32[]{:S(2)}, u32[]{:S(2)}) collective-permute-start(bf16[1,128,1152]{2,1,0:T(8,128)(2,1)S(1)} %add_convert_fusion.12), channel_id=1, source_target_pairs={{0,16},{2,18},{4,20},{6,22},{8,24},{10,26},{12,28},{14,30},{16,0},... | collective-permute-start | bytes 884744 | tf_op jit(solution)/shard_map/ppermute | solution.py:12
  353.6 12.6 %collective-permute-start.21 = (bf16[512,1024]{1,0:T(8,128)(2,1)}, bf16[512,1024]{1,0:T(8,128)(2,1)}, u32[]{:S(2)}, u32[]{:S(2)}) collective-permute-start(bf16[512,1024]{1,0:T(8,128)(2,1)} %get-tuple-element.19), channel_id=1, source_target_pairs={{0,2},{2,0},{4,6},{6,4},{8,10},{10,8},{12,14},{14,12},{16,18},{18,... | collective-permute-start | bytes 3145736 | tf_op jit(solution)/shard_map/ppermute | solution.py:12
  355.9 5.7 %collective-permute-start.22 = (bf16[4,2,1024]{2,1,0:T(2,128)(2,1)S(1)}, bf16[4,2,1024]{2,1,0:T(2,128)(2,1)S(1)}, u32[]{:S(2)}, u32[]{:S(2)}) collective-permute-start(bf16[4,2,1024]{2,1,0:T(2,128)(2,1)S(1)} %slice.515), channel_id=1, source_target_pairs={{4,0},{8,4},{12,8},{16,12},{20,16},{24,20},{28,24},{5,1},{9,5},{13... | collective-permute-start | bytes 49160 | tf_op jit(solution)/shard_map/ppermute | solution.py:12
  357.2 4.4 collective-permute-start.23
  358.5 4.7 collective-permute-start.41
  359.1 5.1 collective-permute-start.37
  361.6 3.5 collective-permute-start.33
  381.5 48.4 %collective-permute-start.25 = (bf16[8,128,1024]{2,1,0:T(8,128)(2,1)S(1)}, bf16[8,128,1024]{2,1,0:T(8,128)(2,1)S(1)}, u32[]{:S(2)}, u32[]{:S(2)}) collective-permute-start(bf16[8,128,1024]{2,1,0:T(8,128)(2,1)S(1)} %dynamic-slice_dynamic-update-slice_fusion), channel_id=1, source_target_pairs={{0,1},{1,0},{2,3},{3,2},{4,5},{5,4},{6,7},{7,6},{8,9},{9,8},{10,11... | collective-permute-start | bytes 6291464 | tf_op jit(solution)/shard_map/ppermute | solution.py:24
  388.5 45.7 %collective-permute-start.24 = (bf16[512,1024]{1,0:T(8,128)(2,1)S(1)}, bf16[512,1024]{1,0:T(8,128)(2,1)S(1)}, u32[]{:S(2)}, u32[]{:S(2)}) collective-permute-start(bf16[512,1024]{1,0:T(8,128)(2,1)S(1)} %slice.522), channel_id=1, source_target_pairs={{0,2},{2,0},{4,6},{6,4},{8,10},{10,8},{12,14},{14,12},{16,18},{18,... | collective-permute-start | bytes 3145736 | tf_op jit(solution)/shard_map/ppermute | solution.py:12
  389.7 80.8 %copy-start.11 = (bf16[8,128,1024]{2,1,0:T(8,128)(2,1)}, bf16[8,128,1024]{2,1,0:T(8,128)(2,1)S(1)}, u32[]{:S(2)}) copy-start(bf16[8,128,1024]{2,1,0:T(8,128)(2,1)S(1)} %pad_maximum_fusion.6) | copy-start | bytes 6291460
  429.9 40.7 %copy-start.17 = (bf16[8,128,1024]{2,1,0:T(8,128)(2,1)}, bf16[8,128,1024]{2,1,0:T(8,128)(2,1)S(1)}, u32[]{:S(2)}) copy-start(bf16[8,128,1024]{2,1,0:T(8,128)(2,1)S(1)} %collective-permute-done.25) | copy-start | bytes 6291460
  430.3 26.4 %collective-permute-start.26 = (bf16[4,128,1024]{2,1,0:T(8,128)(2,1)S(1)}, bf16[4,128,1024]{2,1,0:T(8,128)(2,1)S(1)}, u32[]{:S(2)}, u32[]{:S(2)}) collective-permute-start(bf16[4,128,1024]{2,1,0:T(8,128)(2,1)S(1)} %add_convert_fusion.2), channel_id=1, source_target_pairs={{0,4},{2,6},{4,0},{6,2},{8,12},{10,14},{12,8},{14,10},{16,20},{18,... | collective-permute-start | bytes 3145736 | tf_op jit(solution)/shard_map/ppermute | solution.py:12
  457.0 13.5 %collective-permute-start.27 = (bf16[2,128,1024]{2,1,0:T(8,128)(2,1)S(1)}, bf16[2,128,1024]{2,1,0:T(8,128)(2,1)S(1)}, u32[]{:S(2)}, u32[]{:S(2)}) collective-permute-start(bf16[2,128,1024]{2,1,0:T(8,128)(2,1)S(1)} %add_convert_fusion.9), channel_id=1, source_target_pairs={{0,8},{2,10},{4,12},{6,14},{8,0},{10,2},{12,4},{14,6},{16,24},{18,... | collective-permute-start | bytes 1572872 | tf_op jit(solution)/shard_map/ppermute | solution.py:12
  471.3 41.4 %collective-permute-start.28 = (bf16[1,128,1024]{2,1,0:T(8,128)(2,1)S(1)}, bf16[1,128,1024]{2,1,0:T(8,128)(2,1)S(1)}, u32[]{:S(2)}, u32[]{:S(2)}) collective-permute-start(bf16[1,128,1024]{2,1,0:T(8,128)(2,1)S(1)} %add_convert_fusion.13), channel_id=1, source_target_pairs={{0,16},{2,18},{4,20},{6,22},{8,24},{10,26},{12,28},{14,30},{16,0},... | collective-permute-start | bytes 786440 | tf_op jit(solution)/shard_map/ppermute | solution.py:12
  514.3 1.4 collective-permute-start.29
  (49 other events, 310.7 us)
where the time goes:
time: 524 us; the launch traced here: 518 us
  waiting for transfers between devices  232 us (44%)
  matrix products  122 us (23%)
  other arithmetic  46 us (9%)
  blocking collectives  40.1 us (8%)
  local copies, waits for them, and re-layouts  38.7 us (7%)
  starting transfers between devices  36 us (7%)
    ppermute x34, waiting for transfers between devices, over_seq(): return lax.ppermute(block, 'seq', route)  144 us
    ppermute x8, waiting for transfers between devices, swap_pair(): return lax.ppermute(block, 'wshard', [(0, 1), (1, 0)])  88.6 us
    dot_general x9, matrix products, mm_nt(): lax.dot_general(left, right, (((1,), (1,)), ((), ())), preferred_element_...  50.2 us
    psum x1, blocking collectives, local(): lax.psum(jnp.concatenate([spread, grad_gain_mix[None], grad_gain_ffn[None...  40.1 us
    dot_general x9, matrix products, mm(): return jnp.dot(left, right, preferred_element_type=F32)  39.3 us
    dot_general x5, matrix products, mm_tn(): lax.dot_general(left, right, (((0,), (0,)), ((), ())), preferred_element_...  32.9 us
    ppermute x34, starting transfers between devices, over_seq(): return lax.ppermute(block, 'seq', route)  26.3 us
    unnamed x125, local copies, waits for them, and re-layouts  18.5 us
  transfers between devices with their start and end apart: 42, of which 15 were waited for; matrix products, arithmetic and copies ran while one was open for 33% of the time, Pallas kernels for 0%

commit v1 on v0

--- a/solution.py
+++ b/solution.py
@@ -345,8 +345,10 @@
         spread, grad_taps[:, features:], (1 - pair) * half_width + core * features, 1
     )
     sums = lax.psum(
-        jnp.concatenate([spread, grad_gain_mix[None], grad_gain_ffn[None]], axis=0),
-        ("seq", "wshard"),
+        lax.psum(
+            jnp.concatenate([spread, grad_gain_mix[None], grad_gain_ffn[None]], axis=0), "wshard"
+        ),
+        "seq",
     )
     sums = lax.dynamic_slice_in_dim(sums, pair * half_width, half_width, 1)
     return (

time: 524 us -> 549 us (1.048)
  blocking collectives: 40.1 us -> 65.3 us
    psum x0 -> x1, blocking collectives: none -> 57.6 us  [local(): lax.psum(lax.psum(jnp.concatenate([spread, grad_gain_mix[None], grad_gain...]
    psum x1, blocking collectives: 40.1 us -> 7.63 us  [local(): lax.psum(jnp.concatenate([spread, grad_gain_mix[None], grad_gain_ffn[None...]
  transfers between devices with their start and end apart: 42 -> 42, of which waited for: 15 -> 15; matrix products, arithmetic and copies ran while one was open for 33% -> 31% of each run, Pallas kernels for 0% -> 0%
where the time goes in v1:
time: 549 us; the launch traced here: 543 us
  waiting for transfers between devices  232 us (42%)
  matrix products  122 us (22%)
  blocking collectives  65.3 us (12%)
  other arithmetic  46 us (8%)
  local copies, waits for them, and re-layouts  38.6 us (7%)
  starting transfers between devices  35.8 us (7%)
    ppermute x34, waiting for transfers between devices, over_seq(): return lax.ppermute(block, 'seq', route)  144 us
    ppermute x8, waiting for transfers between devices, swap_pair(): return lax.ppermute(block, 'wshard', [(0, 1), (1, 0)])  88.7 us
    psum x1, blocking collectives, local(): lax.psum(lax.psum(jnp.concatenate([spread, grad_gain_mix[None], grad_gain...  57.6 us
    dot_general x9, matrix products, mm_nt(): lax.dot_general(left, right, (((1,), (1,)), ((), ())), preferred_element_...  50.3 us
    dot_general x9, matrix products, mm(): return jnp.dot(left, right, preferred_element_type=F32)  39.3 us
    dot_general x5, matrix products, mm_tn(): lax.dot_general(left, right, (((0,), (0,)), ((), ())), preferred_element_...  32.9 us
    ppermute x34, starting transfers between devices, over_seq(): return lax.ppermute(block, 'seq', route)  26.3 us
    unnamed x125, local copies, waits for them, and re-layouts  18.5 us
  transfers between devices with their start and end apart: 42, of which 15 were waited for; matrix products, arithmetic and copies ran while one was open for 31% of the time, Pallas kernels for 0%

profile of v1, /device:TPU:0, one launch (start us, length us, event | category | flops | bytes accessed | tf_op | source)
XLA Modules:
  0.0 542.7 jit_solution(3535838593089581746)
XLA Ops:
  0.7 3.2 copy.56
  9.0 3.0 collective-permute-start.2
  12.7 4.7 collective-permute-start.7
  21.6 25.2 %collective-permute-done.1 = bf16[5,512]{1,0:T(8,128)(2,1)S(1)} collective-permute-done((bf16[5,512]{1,0:T(8,128)(2,1)S(1)}, bf16[5,512]{1,0:T(8,128)(2,1)S(1)}, u32[]{:S(2)}, u32[]{:S(2)}) %collective-permute-start.1) | collective-permute-done | bytes 5152 | tf_op jit(solution)/shard_map/ppermute | solution.py:24
  52.9 1.9 fusion.78
  54.8 2.0 fusion.77
  60.6 2.4 fusion.86
  63.7 5.4 fusion.73
  73.1 4.2 convolution_convert_fusion.4
  79.7 23.4 %collective-permute-done.17 = bf16[512,1024]{1,0:T(8,128)(2,1)} collective-permute-done((bf16[512,1024]{1,0:T(8,128)(2,1)}, bf16[512,1024]{1,0:T(8,128)(2,1)}, u32[]{:S(2)}, u32[]{:S(2)}) %collective-permute-start.17) | collective-permute-done | bytes 1048608 | tf_op jit(solution)/shard_map/ppermute | solution.py:24
  103.1 3.6 fusion.121
  108.7 2.7 multiply_reduce_fusion
  113.5 4.5 fusion.61
  118.0 4.5 fusion.69
  122.5 9.8 %multiply_convert_fusion.2 = (bf16[1024,1152]{1,0:T(8,128)(2,1)S(1)}, bf16[1024,1152]{1,0:T(8,128)(2,1)}, bf16[1024,1152]{1,0:T(8,128)(2,1)}) fusion(f32[1024,1152]{1,0:T(8,128)} %fusion.69, f32[1024,1152]{1,0:T(8,128)} %fusion.61, bf16[2304,1024]{1,0:T(8,128)(2,1)S(1)} %bitcast.220, s32[]{:T(128)S(6)} %select_n.227, ...), kind=kOutput, calls=%fused_computation.14 | convolution fusion | flops 2437808128 | bytes 20971524 | tf_op jit(solution)/shard_map/dot_general | solution.py:40
  132.3 6.1 %fusion.65 = f32[1024,1024]{1,0:T(8,128)S(1)} fusion(bf16[1024,1152]{1,0:T(8,128)(2,1)} %get-tuple-element.24, bf16[1024,2304]{1,0:T(8,128)(2,1)} %param.16, s32[]{:T(128)S(6)} %select_n.227), kind=kOutput, calls=%fused_computation.113 | convolution fusion | flops 2415919104 | bytes 8912900 | tf_op jit(solution)/shard_map/dot_general | solution.py:40
  138.8 5.0 add_convert_fusion.1
  145.1 3.3 convolution_convert_fusion.2
  149.7 4.5 fusion.59
  154.1 4.5 fusion.67
  158.6 11.5 %multiply_convert_fusion = (bf16[1024,1152]{1,0:T(8,128)(2,1)S(1)}, bf16[1024,1152]{1,0:T(8,128)(2,1)}, bf16[1024,1152]{1,0:T(8,128)(2,1)}) fusion(f32[1024,1152]{1,0:T(8,128)} %fusion.67, f32[1024,1152]{1,0:T(8,128)} %fusion.59, bf16[2304,1024]{1,0:T(8,128)(2,1)} %param.18, s32[]{:T(128)S(6)} %select_n.227, bf16[512,1024]{1,0:T(8,128)(2,1)} %collective-permute-done.18, ...), kind=kOutput, calls=%fused_computation.12 | convolution fusion | flops 2437808128 | bytes 20971524 | tf_op jit(solution)/shard_map/dot_general | solution.py:40
  170.1 6.1 %convolution_convert_fusion.1 = bf16[1024,1024]{1,0:T(8,128)(2,1)S(1)} fusion(bf16[1024,1152]{1,0:T(8,128)(2,1)} %get-tuple-element.28, bf16[2304,1024]{1,0:T(8,128)(2,1)} %param.18, s32[]{:T(128)S(6)} %select_n.227), kind=kOutput, calls=%fused_computation.96 | convolution fusion | flops 2416967680 | bytes 6815748 | tf_op jit(solution)/shard_map/dot_general | solution.py:32
  177.6 4.6 fusion.63
  182.2 3.6 add_convert_fusion
  187.7 9.3 %fusion.21 = bf16[1024,1152]{1,0:T(8,128)(2,1)S(1)} fusion(bf16[1024,1152]{1,0:T(8,128)(2,1)} %get-tuple-element.28, bf16[1024,1152]{1,0:T(8,128)(2,1)} %get-tuple-element.25, bf16[512,1024]{1,0:T(8,128)(2,1)} %collective-permute-done.18, bf16[512,1024]{1,0:T(8,128)(2,1)} %collective-permute-done.17, bf16[512,1024]{1,0:T(8,128)(2,1)} %collective-permute-done.15, ...), kind=kOutput, calls=%fused_computation.37 | convolution fusion | flops 4859232256 | bytes 11272192 | tf_op jit(solution)/shard_map/dot_general | solution.py:36
  199.9 8.2 %fusion.26 = bf16[1024,1152]{1,0:T(8,128)(2,1)S(1)} fusion(bf16[1024,1152]{1,0:T(8,128)(2,1)} %copy-done.38, bf16[1024,1152]{1,0:T(8,128)(2,1)} %copy-done.37, bf16[512,1024]{1,0:T(8,128)(2,1)S(1)} %collective-permute-done.12, bf16[512,1024]{1,0:T(8,128)(2,1)S(1)} %collective-permute-done.11, bf16[1024,1024]{1,0:T(8,128)(2,1)S(1)} %multiply_convert_fusion.6), kind=kOutput, calls=%fused_computation.38 | convolution fusion | flops 4855037952 | bytes 11272192 | tf_op jit(solution)/shard_map/dot_general | solution.py:36
  210.2 8.8 %fusion.29 = bf16[1024,1152]{1,0:T(8,128)(2,1)S(1)} fusion(bf16[1024,1152]{1,0:T(8,128)(2,1)} %get-tuple-element.27, bf16[1024,1152]{1,0:T(8,128)(2,1)} %get-tuple-element.24, bf16[512,1024]{1,0:T(8,128)(2,1)} %copy-done.24, bf16[512,1024]{1,0:T(8,128)(2,1)} %copy-done.23, bf16[1024,1024]{1,0:T(8,128)(2,1)S(1)} %multiply_convert_fusion.6), kind=kOutput, calls=%fused_computation.39 | convolution fusion | flops 4855037952 | bytes 11272192 | tf_op jit(solution)/shard_map/dot_general | solution.py:36
  229.3 23.5 %collective-permute-done.34 = bf16[4,128,1152]{2,1,0:T(8,128)(2,1)} collective-permute-done((bf16[4,128,1152]{2,1,0:T(8,128)(2,1)}, bf16[4,128,1152]{2,1,0:T(8,128)(2,1)}, u32[]{:S(2)}, u32[]{:S(2)}) %collective-permute-start.34) | collective-permute-done | bytes 1179680 | tf_op jit(solution)/shard_map/ppermute | solution.py:12
  255.6 21.7 %collective-permute-done.30 = bf16[4,128,1152]{2,1,0:T(8,128)(2,1)S(1)} collective-permute-done((bf16[4,128,1152]{2,1,0:T(8,128)(2,1)S(1)}, bf16[4,128,1152]{2,1,0:T(8,128)(2,1)S(1)}, u32[]{:S(2)}, u32[]{:S(2)}) %collective-permute-start.30) | collective-permute-done | bytes 1179680 | tf_op jit(solution)/shard_map/ppermute | solution.py:12
  280.6 12.9 %collective-permute-done.35 = bf16[2,128,1152]{2,1,0:T(8,128)(2,1)S(1)} collective-permute-done((bf16[2,128,1152]{2,1,0:T(8,128)(2,1)S(1)}, bf16[2,128,1152]{2,1,0:T(8,128)(2,1)S(1)}, u32[]{:S(2)}, u32[]{:S(2)}) %collective-permute-start.35) | collective-permute-done | bytes 589856 | tf_op jit(solution)/shard_map/ppermute | solution.py:12
  295.2 9.4 %collective-permute-done.31 = bf16[2,128,1152]{2,1,0:T(8,128)(2,1)S(1)} collective-permute-done((bf16[2,128,1152]{2,1,0:T(8,128)(2,1)S(1)}, bf16[2,128,1152]{2,1,0:T(8,128)(2,1)S(1)}, u32[]{:S(2)}, u32[]{:S(2)}) %collective-permute-start.31) | collective-permute-done | bytes 589856 | tf_op jit(solution)/shard_map/ppermute | solution.py:12
  304.6 2.6 collective-permute-start.40
  307.3 11.9 %collective-permute-done.40 = bf16[1,128,1152]{2,1,0:T(8,128)(2,1)S(1)} collective-permute-done((bf16[1,128,1152]{2,1,0:T(8,128)(2,1)S(1)}, bf16[1,128,1152]{2,1,0:T(8,128)(2,1)S(1)}, u32[]{:S(2)}, u32[]{:S(2)}) %collective-permute-start.40) | collective-permute-done | bytes 294944 | tf_op jit(solution)/shard_map/ppermute | solution.py:12
  320.3 13.9 %collective-permute-done.36 = bf16[1,128,1152]{2,1,0:T(8,128)(2,1)S(1)} collective-permute-done((bf16[1,128,1152]{2,1,0:T(8,128)(2,1)S(1)}, bf16[1,128,1152]{2,1,0:T(8,128)(2,1)S(1)}, u32[]{:S(2)}, u32[]{:S(2)}) %collective-permute-start.36) | collective-permute-done | bytes 294944 | tf_op jit(solution)/shard_map/ppermute | solution.py:12
  336.8 11.6 %collective-permute-done.32 = bf16[1,128,1152]{2,1,0:T(8,128)(2,1)S(1)} collective-permute-done((bf16[1,128,1152]{2,1,0:T(8,128)(2,1)S(1)}, bf16[1,128,1152]{2,1,0:T(8,128)(2,1)S(1)}, u32[]{:S(2)}, u32[]{:S(2)}) %collective-permute-start.32) | collective-permute-done | bytes 294944 | tf_op jit(solution)/shard_map/ppermute | solution.py:12
  349.5 4.0 fusion.122
  359.0 2.6 collective-permute-done.22
  366.2 4.6 multiply_reduce_fusion.6
  373.9 2.9 convolution_convert_fusion.5
  377.0 3.7 convolution_convert_fusion
  384.7 3.7 convolution_convert_fusion.3
  389.8 40.1 %collective-permute-done.25 = bf16[8,128,1024]{2,1,0:T(8,128)(2,1)S(1)} collective-permute-done((bf16[8,128,1024]{2,1,0:T(8,128)(2,1)S(1)}, bf16[8,128,1024]{2,1,0:T(8,128)(2,1)S(1)}, u32[]{:S(2)}, u32[]{:S(2)}) %collective-permute-start.25) | collective-permute-done | bytes 2097184 | tf_op jit(solution)/shard_map/ppermute | solution.py:24
  430.3 3.0 collective-permute-start.26
  435.1 21.7 %collective-permute-done.26 = bf16[4,128,1024]{2,1,0:T(8,128)(2,1)S(1)} collective-permute-done((bf16[4,128,1024]{2,1,0:T(8,128)(2,1)S(1)}, bf16[4,128,1024]{2,1,0:T(8,128)(2,1)S(1)}, u32[]{:S(2)}, u32[]{:S(2)}) %collective-permute-start.26) | collective-permute-done | bytes 1048608 | tf_op jit(solution)/shard_map/ppermute | solution.py:12
  457.2 2.0 multiply_add_fusion
  459.2 11.3 %collective-permute-done.27 = bf16[2,128,1024]{2,1,0:T(8,128)(2,1)S(1)} collective-permute-done((bf16[2,128,1024]{2,1,0:T(8,128)(2,1)S(1)}, bf16[2,128,1024]{2,1,0:T(8,128)(2,1)S(1)}, u32[]{:S(2)}, u32[]{:S(2)}) %collective-permute-start.27) | collective-permute-done | bytes 524320 | tf_op jit(solution)/shard_map/ppermute | solution.py:12
  471.4 7.6 %psum.14 = f32[5,1024]{1,0:T(8,128)S(1)} all-reduce(f32[5,1024]{1,0:T(8,128)S(1)} %pad_maximum_fusion.23), channel_id=1, replica_groups=mesh['seq'=16,'wshard'=2] {'wshard'}, use_global_device_ids=true, to_apply=%region_10.11 | all-reduce | flops 5120 | bytes 40960 | tf_op jit(solution)/shard_map/psum | solution.py:348
  479.0 57.6 %psum.15 = f32[5,1024]{1,0:T(8,128)S(1)} all-reduce(f32[5,1024]{1,0:T(8,128)S(1)} %psum.14), channel_id=1, replica_groups=mesh['seq'=16,'wshard'=2] {'seq'}, use_global_device_ids=true, to_apply=%region_11.12 | all-reduce | flops 5120 | bytes 40960 | tf_op jit(solution)/shard_map/psum | solution.py:347
  (327 shorter events, 92.5 us)
Async XLA Ops:
  5.7 41.8 %collective-permute-start.5 = (bf16[4,2,1152]{2,0,1:T(4,128)(2,1)S(1)}, bf16[4,2,1152]{2,0,1:T(4,128)(2,1)S(1)}, u32[]{:S(2)}, u32[]{:S(2)}) collective-permute-start(bf16[4,2,1152]{2,0,1:T(4,128)(2,1)S(1)} %get-tuple-element.69), channel_id=1, source_target_pairs={{4,0},{8,4},{12,8},{16,12},{20,16},{24,20},{28,24},{5,1},{9,5},{13... | collective-permute-start | bytes 55304 | tf_op jit(solution)/shard_map/ppermute | solution.py:12
  7.0 41.0 %collective-permute-start.6 = (bf16[4,2,1152]{2,0,1:T(4,128)(2,1)S(1)}, bf16[4,2,1152]{2,0,1:T(4,128)(2,1)S(1)}, u32[]{:S(2)}, u32[]{:S(2)}) collective-permute-start(bf16[4,2,1152]{2,0,1:T(4,128)(2,1)S(1)} %get-tuple-element.69), channel_id=1, source_target_pairs={{4,2},{8,6},{12,10},{16,14},{20,18},{24,22},{28,26},{5,3},{9,7},{1... | collective-permute-start | bytes 55304 | tf_op jit(solution)/shard_map/ppermute | solution.py:12
  9.0 38.6 %copy-start.6 = (bf16[4,128,1024]{2,1,0:T(8,128)(2,1)S(1)}, bf16[4,128,1024]{2,1,0:T(8,128)(2,1)}, u32[]{:S(2)}) copy-start(bf16[4,128,1024]{2,1,0:T(8,128)(2,1)} %param.11) | copy-start | bytes 3145732
  9.0 42.0 %collective-permute-start.2 = (bf16[3,1024,256]{2,1,0:T(8,128)(2,1)}, bf16[3,1024,256]{2,1,0:T(8,128)(2,1)}, u32[]{:S(2)}, u32[]{:S(2)}) collective-permute-start(bf16[3,1024,256]{2,1,0:T(8,128)(2,1)} %dynamic-slice_bitcast_fusion), channel_id=1, source_target_pairs={{0,1},{1,0},{2,3},{3,2},{4,5},{5,4},{6,7},{7,6},{8,9},{9,8},{10,11... | collective-permute-start | bytes 4718600 | tf_op jit(solution)/shard_map/ppermute | solution.py:24
  11.9 37.5 %collective-permute-start.3 = (bf16[4,2,1152]{2,0,1:T(4,128)(2,1)S(1)}, bf16[4,2,1152]{2,0,1:T(4,128)(2,1)S(1)}, u32[]{:S(2)}, u32[]{:S(2)}) collective-permute-start(bf16[4,2,1152]{2,0,1:T(4,128)(2,1)S(1)} %get-tuple-element.68), channel_id=1, source_target_pairs={{2,4},{6,8},{10,12},{14,16},{18,20},{22,24},{26,28},{3,5},{7,9},{1... | collective-permute-start | bytes 55304 | tf_op jit(solution)/shard_map/ppermute | solution.py:12
  12.7 8.6 %collective-permute-start.7 = (s32[4,128]{0,1:T(8,128)S(1)}, s32[4,128]{0,1:T(8,128)S(1)}, u32[]{:S(2)}, u32[]{:S(2)}) collective-permute-start(s32[4,128]{0,1:T(8,128)S(1)} %copy.57), channel_id=1, source_target_pairs={{0,2},{2,0},{4,6},{6,4},{8,10},{10,8},{12,14},{14,12},{16,18},{18,... | collective-permute-start | bytes 6152 | tf_op jit(solution)/shard_map/ppermute | solution.py:12
  21.3 25.4 %collective-permute-start.1 = (bf16[5,512]{1,0:T(8,128)(2,1)S(1)}, bf16[5,512]{1,0:T(8,128)(2,1)S(1)}, u32[]{:S(2)}, u32[]{:S(2)}) collective-permute-start(bf16[5,512]{1,0:T(8,128)(2,1)S(1)} %pad_maximum_fusion.26), channel_id=1, source_target_pairs={{0,1},{1,0},{2,3},{3,2},{4,5},{5,4},{6,7},{7,6},{8,9},{9,8},{10,11... | collective-permute-start | bytes 15368 | tf_op jit(solution)/shard_map/ppermute | solution.py:24
  46.7 2.7 collective-permute-start.4
  47.5 2.9 collective-permute-start
  48.0 25.1 %collective-permute-start.8 = (bf16[256,1024]{1,0:T(8,128)(2,1)}, bf16[256,1024]{1,0:T(8,128)(2,1)}, u32[]{:S(2)}, u32[]{:S(2)}) collective-permute-start(bf16[256,1024]{1,0:T(8,128)(2,1)} %constant_dynamic-slice_fusion.25), channel_id=1, source_target_pairs={{0,1},{1,0},{2,3},{3,2},{4,5},{5,4},{6,7},{7,6},{8,9},{9,8},{10,11... | collective-permute-start | bytes 1572872 | tf_op jit(solution)/shard_map/ppermute | solution.py:24
  50.9 28.1 %copy-start.31 = (f32[1024]{0:T(1024)}, f32[1024]{0:T(1024)S(1)}, u32[]{:S(2)}) copy-start(f32[1024]{0:T(1024)S(1)} %add_rsqrt_fusion.1) | copy-start | bytes 12292
  77.2 29.5 %collective-permute-start.9 = (bf16[1024,1024]{1,0:T(8,128)(2,1)}, bf16[1024,1024]{1,0:T(8,128)(2,1)}, u32[]{:S(2)}, u32[]{:S(2)}) collective-permute-start(bf16[1024,1024]{1,0:T(8,128)(2,1)} %convolution_convert_fusion.4), channel_id=1, source_target_pairs={{0,2},{2,0},{4,6},{6,4},{8,10},{10,8},{12,14},{14,12},{16,18},{18,... | collective-permute-start | bytes 6291464 | tf_op jit(solution)/shard_map/ppermute | solution.py:12
  77.4 25.7 %collective-permute-start.17 = (bf16[512,1024]{1,0:T(8,128)(2,1)}, bf16[512,1024]{1,0:T(8,128)(2,1)}, u32[]{:S(2)}, u32[]{:S(2)}) collective-permute-start(bf16[512,1024]{1,0:T(8,128)(2,1)} %bitcast.18), channel_id=1, source_target_pairs={{0,1},{1,0},{2,3},{3,2},{4,5},{5,4},{6,7},{7,6},{8,9},{9,8},{10,11... | collective-permute-start | bytes 3145736 | tf_op jit(solution)/shard_map/ppermute | solution.py:24
  78.9 43.6 %collective-permute-start.15 = (bf16[512,1024]{1,0:T(8,128)(2,1)}, bf16[512,1024]{1,0:T(8,128)(2,1)}, u32[]{:S(2)}, u32[]{:S(2)}) collective-permute-start(bf16[512,1024]{1,0:T(8,128)(2,1)} %bitcast.18), channel_id=1, source_target_pairs={{0,2},{2,0},{4,6},{6,4},{8,10},{10,8},{12,14},{14,12},{16,18},{18,... | collective-permute-start | bytes 3145736 | tf_op jit(solution)/shard_map/ppermute | solution.py:12
  103.1 55.5 %collective-permute-start.18 = (bf16[512,1024]{1,0:T(8,128)(2,1)}, bf16[512,1024]{1,0:T(8,128)(2,1)}, u32[]{:S(2)}, u32[]{:S(2)}) collective-permute-start(bf16[512,1024]{1,0:T(8,128)(2,1)} %collective-permute-done.17), channel_id=1, source_target_pairs={{0,2},{2,0},{4,6},{6,4},{8,10},{10,8},{12,14},{14,12},{16,18},{18,... | collective-permute-start | bytes 3145736 | tf_op jit(solution)/shard_map/ppermute | solution.py:12
  111.9 26.6 %collective-permute-start.11 = (bf16[512,1024]{1,0:T(8,128)(2,1)S(1)}, bf16[512,1024]{1,0:T(8,128)(2,1)S(1)}, u32[]{:S(2)}, u32[]{:S(2)}) collective-permute-start(bf16[512,1024]{1,0:T(8,128)(2,1)S(1)} %slice.503), channel_id=1, source_target_pairs={{0,1},{1,0},{2,3},{3,2},{4,5},{5,4},{6,7},{7,6},{8,9},{9,8},{10,11... | collective-permute-start | bytes 3145736 | tf_op jit(solution)/shard_map/ppermute | solution.py:24
  138.5 61.4 %copy-start.23 = (bf16[512,1024]{1,0:T(8,128)(2,1)}, bf16[512,1024]{1,0:T(8,128)(2,1)S(1)}, u32[]{:S(2)}) copy-start(bf16[512,1024]{1,0:T(8,128)(2,1)S(1)} %collective-permute-done.11) | copy-start | bytes 3145732
  138.5 11.0 %collective-permute-start.12 = (bf16[512,1024]{1,0:T(8,128)(2,1)S(1)}, bf16[512,1024]{1,0:T(8,128)(2,1)S(1)}, u32[]{:S(2)}, u32[]{:S(2)}) collective-permute-start(bf16[512,1024]{1,0:T(8,128)(2,1)S(1)} %collective-permute-done.11), channel_id=1, source_target_pairs={{0,2},{2,0},{4,6},{6,4},{8,10},{10,8},{12,14},{14,12},{16,18},{18,... | collective-permute-start | bytes 3145736 | tf_op jit(solution)/shard_map/ppermute | solution.py:12
  144.8 203.7 %collective-permute-start.16 = (bf16[512,1024]{1,0:T(8,128)(2,1)}, bf16[512,1024]{1,0:T(8,128)(2,1)S(1)}, u32[]{:S(2)}, u32[]{:S(2)}) collective-permute-start(bf16[512,1024]{1,0:T(8,128)(2,1)} %slice.507), channel_id=1, source_target_pairs={{0,2},{2,0},{4,6},{6,4},{8,10},{10,8},{12,14},{14,12},{16,18},{18,... | collective-permute-start | bytes 3145736 | tf_op jit(solution)/shard_map/ppermute | solution.py:12
  149.5 50.4 %copy-start.24 = (bf16[512,1024]{1,0:T(8,128)(2,1)}, bf16[512,1024]{1,0:T(8,128)(2,1)S(1)}, u32[]{:S(2)}) copy-start(bf16[512,1024]{1,0:T(8,128)(2,1)S(1)} %collective-permute-done.12) | copy-start | bytes 3145732
  177.3 42.1 %collective-permute-start.13 = (bf16[512,1024]{1,0:T(8,128)(2,1)}, bf16[512,1024]{1,0:T(8,128)(2,1)}, u32[]{:S(2)}, u32[]{:S(2)}) collective-permute-start(bf16[512,1024]{1,0:T(8,128)(2,1)} %slice.505), channel_id=1, source_target_pairs={{0,2},{2,0},{4,6},{6,4},{8,10},{10,8},{12,14},{14,12},{16,18},{18,... | collective-permute-start | bytes 3145736 | tf_op jit(solution)/shard_map/ppermute | solution.py:12
  187.4 35.1 %collective-permute-start.19 = (bf16[512,1024]{1,0:T(8,128)(2,1)}, bf16[512,1024]{1,0:T(8,128)(2,1)}, u32[]{:S(2)}, u32[]{:S(2)}) collective-permute-start(bf16[512,1024]{1,0:T(8,128)(2,1)} %slice.509), channel_id=1, source_target_pairs={{0,2},{2,0},{4,6},{6,4},{8,10},{10,8},{12,14},{14,12},{16,18},{18,... | collective-permute-start | bytes 3145736 | tf_op jit(solution)/shard_map/ppermute | solution.py:12
  198.4 29.1 %collective-permute-start.38 = (bf16[4,128,1152]{2,1,0:T(8,128)(2,1)}, bf16[4,128,1152]{2,1,0:T(8,128)(2,1)}, u32[]{:S(2)}, u32[]{:S(2)}) collective-permute-start(bf16[4,128,1152]{2,1,0:T(8,128)(2,1)} %pad_maximum_fusion.16), channel_id=1, source_target_pairs={{0,4},{2,6},{4,0},{6,2},{8,12},{10,14},{12,8},{14,10},{16,20},{18,... | collective-permute-start | bytes 3538952 | tf_op jit(solution)/shard_map/ppermute | solution.py:12
  209.7 43.1 %collective-permute-start.34 = (bf16[4,128,1152]{2,1,0:T(8,128)(2,1)}, bf16[4,128,1152]{2,1,0:T(8,128)(2,1)}, u32[]{:S(2)}, u32[]{:S(2)}) collective-permute-start(bf16[4,128,1152]{2,1,0:T(8,128)(2,1)} %pad_maximum_fusion.15), channel_id=1, source_target_pairs={{0,4},{2,6},{4,0},{6,2},{8,12},{10,14},{12,8},{14,10},{16,20},{18,... | collective-permute-start | bytes 3538952 | tf_op jit(solution)/shard_map/ppermute | solution.py:12
  220.2 129.3 %collective-permute-start.10 = (bf16[512,1024]{1,0:T(8,128)(2,1)S(1)}, bf16[512,1024]{1,0:T(8,128)(2,1)S(1)}, u32[]{:S(2)}, u32[]{:S(2)}) collective-permute-start(bf16[512,1024]{1,0:T(8,128)(2,1)S(1)} %copy-done.22), channel_id=1, source_target_pairs={{0,2},{2,0},{4,6},{6,4},{8,10},{10,8},{12,14},{14,12},{16,18},{18,... | collective-permute-start | bytes 3145736 | tf_op jit(solution)/shard_map/ppermute | solution.py:12
  222.5 54.7 %collective-permute-start.30 = (bf16[4,128,1152]{2,1,0:T(8,128)(2,1)S(1)}, bf16[4,128,1152]{2,1,0:T(8,128)(2,1)S(1)}, u32[]{:S(2)}, u32[]{:S(2)}) collective-permute-start(bf16[4,128,1152]{2,1,0:T(8,128)(2,1)S(1)} %pad_maximum_fusion.14), channel_id=1, source_target_pairs={{0,4},{2,6},{4,0},{6,2},{8,12},{10,14},{12,8},{14,10},{16,20},{18,... | collective-permute-start | bytes 3538952 | tf_op jit(solution)/shard_map/ppermute | solution.py:12
  227.5 122.0 %collective-permute-start.14 = (bf16[512,1024]{1,0:T(8,128)(2,1)S(1)}, bf16[512,1024]{1,0:T(8,128)(2,1)S(1)}, u32[]{:S(2)}, u32[]{:S(2)}) collective-permute-start(bf16[512,1024]{1,0:T(8,128)(2,1)S(1)} %add_convert_fusion.5), channel_id=1, source_target_pairs={{0,1},{1,0},{2,3},{3,2},{4,5},{5,4},{6,7},{7,6},{8,9},{9,8},{10,11... | collective-permute-start | bytes 3145736 | tf_op jit(solution)/shard_map/ppermute | solution.py:24
  252.8 26.2 %collective-permute-start.39 = (bf16[2,128,1152]{2,1,0:T(8,128)(2,1)S(1)}, bf16[2,128,1152]{2,1,0:T(8,128)(2,1)S(1)}, u32[]{:S(2)}, u32[]{:S(2)}) collective-permute-start(bf16[2,128,1152]{2,1,0:T(8,128)(2,1)S(1)} %add_convert_fusion.6), channel_id=1, source_target_pairs={{0,8},{2,10},{4,12},{6,14},{8,0},{10,2},{12,4},{14,6},{16,24},{18,... | collective-permute-start | bytes 1769480 | tf_op jit(solution)/shard_map/ppermute | solution.py:12
  277.3 16.3 %collective-permute-start.35 = (bf16[2,128,1152]{2,1,0:T(8,128)(2,1)S(1)}, bf16[2,128,1152]{2,1,0:T(8,128)(2,1)S(1)}, u32[]{:S(2)}, u32[]{:S(2)}) collective-permute-start(bf16[2,128,1152]{2,1,0:T(8,128)(2,1)S(1)} %add_convert_fusion.7), channel_id=1, source_target_pairs={{0,8},{2,10},{4,12},{6,14},{8,0},{10,2},{12,4},{14,6},{16,24},{18,... | collective-permute-start | bytes 1769480 | tf_op jit(solution)/shard_map/ppermute | solution.py:12
  279.0 25.6 %collective-permute-start.31 = (bf16[2,128,1152]{2,1,0:T(8,128)(2,1)S(1)}, bf16[2,128,1152]{2,1,0:T(8,128)(2,1)S(1)}, u32[]{:S(2)}, u32[]{:S(2)}) collective-permute-start(bf16[2,128,1152]{2,1,0:T(8,128)(2,1)S(1)} %add_convert_fusion.8), channel_id=1, source_target_pairs={{0,8},{2,10},{4,12},{6,14},{8,0},{10,2},{12,4},{14,6},{16,24},{18,... | collective-permute-start | bytes 1769480 | tf_op jit(solution)/shard_map/ppermute | solution.py:12
  293.5 55.0 %collective-permute-start.20 = (bf16[512,1024]{1,0:T(8,128)(2,1)S(1)}, bf16[512,1024]{1,0:T(8,128)(2,1)S(1)}, u32[]{:S(2)}, u32[]{:S(2)}) collective-permute-start(bf16[512,1024]{1,0:T(8,128)(2,1)S(1)} %add_convert_fusion.3), channel_id=1, source_target_pairs={{0,1},{1,0},{2,3},{3,2},{4,5},{5,4},{6,7},{7,6},{8,9},{9,8},{10,11... | collective-permute-start | bytes 3145736 | tf_op jit(solution)/shard_map/ppermute | solution.py:24
  304.6 14.6 %collective-permute-start.40 = (bf16[1,128,1152]{2,1,0:T(8,128)(2,1)S(1)}, bf16[1,128,1152]{2,1,0:T(8,128)(2,1)S(1)}, u32[]{:S(2)}, u32[]{:S(2)}) collective-permute-start(bf16[1,128,1152]{2,1,0:T(8,128)(2,1)S(1)} %add_convert_fusion.10), channel_id=1, source_target_pairs={{0,16},{2,18},{4,20},{6,22},{8,24},{10,26},{12,28},{14,30},{16,0},... | collective-permute-start | bytes 884744 | tf_op jit(solution)/shard_map/ppermute | solution.py:12
  319.2 15.0 %collective-permute-start.36 = (bf16[1,128,1152]{2,1,0:T(8,128)(2,1)S(1)}, bf16[1,128,1152]{2,1,0:T(8,128)(2,1)S(1)}, u32[]{:S(2)}, u32[]{:S(2)}) collective-permute-start(bf16[1,128,1152]{2,1,0:T(8,128)(2,1)S(1)} %add_convert_fusion.11), channel_id=1, source_target_pairs={{0,16},{2,18},{4,20},{6,22},{8,24},{10,26},{12,28},{14,30},{16,0},... | collective-permute-start | bytes 884744 | tf_op jit(solution)/shard_map/ppermute | solution.py:12
  334.3 14.1 %collective-permute-start.32 = (bf16[1,128,1152]{2,1,0:T(8,128)(2,1)S(1)}, bf16[1,128,1152]{2,1,0:T(8,128)(2,1)S(1)}, u32[]{:S(2)}, u32[]{:S(2)}) collective-permute-start(bf16[1,128,1152]{2,1,0:T(8,128)(2,1)S(1)} %add_convert_fusion.12), channel_id=1, source_target_pairs={{0,16},{2,18},{4,20},{6,22},{8,24},{10,26},{12,28},{14,30},{16,0},... | collective-permute-start | bytes 884744 | tf_op jit(solution)/shard_map/ppermute | solution.py:12
  353.5 12.7 %collective-permute-start.21 = (bf16[512,1024]{1,0:T(8,128)(2,1)}, bf16[512,1024]{1,0:T(8,128)(2,1)}, u32[]{:S(2)}, u32[]{:S(2)}) collective-permute-start(bf16[512,1024]{1,0:T(8,128)(2,1)} %get-tuple-element.19), channel_id=1, source_target_pairs={{0,2},{2,0},{4,6},{6,4},{8,10},{10,8},{12,14},{14,12},{16,18},{18,... | collective-permute-start | bytes 3145736 | tf_op jit(solution)/shard_map/ppermute | solution.py:12
  355.8 5.7 %collective-permute-start.22 = (bf16[4,2,1024]{2,1,0:T(2,128)(2,1)S(1)}, bf16[4,2,1024]{2,1,0:T(2,128)(2,1)S(1)}, u32[]{:S(2)}, u32[]{:S(2)}) collective-permute-start(bf16[4,2,1024]{2,1,0:T(2,128)(2,1)S(1)} %slice.515), channel_id=1, source_target_pairs={{4,0},{8,4},{12,8},{16,12},{20,16},{24,20},{28,24},{5,1},{9,5},{13... | collective-permute-start | bytes 49160 | tf_op jit(solution)/shard_map/ppermute | solution.py:12
  357.1 4.4 collective-permute-start.23
  358.5 4.7 collective-permute-start.41
  359.0 5.2 collective-permute-start.37
  361.5 3.5 collective-permute-start.33
  381.4 48.4 %collective-permute-start.25 = (bf16[8,128,1024]{2,1,0:T(8,128)(2,1)S(1)}, bf16[8,128,1024]{2,1,0:T(8,128)(2,1)S(1)}, u32[]{:S(2)}, u32[]{:S(2)}) collective-permute-start(bf16[8,128,1024]{2,1,0:T(8,128)(2,1)S(1)} %dynamic-slice_dynamic-update-slice_fusion), channel_id=1, source_target_pairs={{0,1},{1,0},{2,3},{3,2},{4,5},{5,4},{6,7},{7,6},{8,9},{9,8},{10,11... | collective-permute-start | bytes 6291464 | tf_op jit(solution)/shard_map/ppermute | solution.py:24
  388.5 45.8 %collective-permute-start.24 = (bf16[512,1024]{1,0:T(8,128)(2,1)S(1)}, bf16[512,1024]{1,0:T(8,128)(2,1)S(1)}, u32[]{:S(2)}, u32[]{:S(2)}) collective-permute-start(bf16[512,1024]{1,0:T(8,128)(2,1)S(1)} %slice.522), channel_id=1, source_target_pairs={{0,2},{2,0},{4,6},{6,4},{8,10},{10,8},{12,14},{14,12},{16,18},{18,... | collective-permute-start | bytes 3145736 | tf_op jit(solution)/shard_map/ppermute | solution.py:12
  389.6 80.9 %copy-start.11 = (bf16[8,128,1024]{2,1,0:T(8,128)(2,1)}, bf16[8,128,1024]{2,1,0:T(8,128)(2,1)S(1)}, u32[]{:S(2)}) copy-start(bf16[8,128,1024]{2,1,0:T(8,128)(2,1)S(1)} %pad_maximum_fusion.6) | copy-start | bytes 6291460
  429.9 40.7 %copy-start.17 = (bf16[8,128,1024]{2,1,0:T(8,128)(2,1)}, bf16[8,128,1024]{2,1,0:T(8,128)(2,1)S(1)}, u32[]{:S(2)}) copy-start(bf16[8,128,1024]{2,1,0:T(8,128)(2,1)S(1)} %collective-permute-done.25) | copy-start | bytes 6291460
  430.3 26.4 %collective-permute-start.26 = (bf16[4,128,1024]{2,1,0:T(8,128)(2,1)S(1)}, bf16[4,128,1024]{2,1,0:T(8,128)(2,1)S(1)}, u32[]{:S(2)}, u32[]{:S(2)}) collective-permute-start(bf16[4,128,1024]{2,1,0:T(8,128)(2,1)S(1)} %add_convert_fusion.2), channel_id=1, source_target_pairs={{0,4},{2,6},{4,0},{6,2},{8,12},{10,14},{12,8},{14,10},{16,20},{18,... | collective-permute-start | bytes 3145736 | tf_op jit(solution)/shard_map/ppermute | solution.py:12
  457.0 13.5 %collective-permute-start.27 = (bf16[2,128,1024]{2,1,0:T(8,128)(2,1)S(1)}, bf16[2,128,1024]{2,1,0:T(8,128)(2,1)S(1)}, u32[]{:S(2)}, u32[]{:S(2)}) collective-permute-start(bf16[2,128,1024]{2,1,0:T(8,128)(2,1)S(1)} %add_convert_fusion.9), channel_id=1, source_target_pairs={{0,8},{2,10},{4,12},{6,14},{8,0},{10,2},{12,4},{14,6},{16,24},{18,... | collective-permute-start | bytes 1572872 | tf_op jit(solution)/shard_map/ppermute | solution.py:12
  471.3 66.6 %collective-permute-start.28 = (bf16[1,128,1024]{2,1,0:T(8,128)(2,1)S(1)}, bf16[1,128,1024]{2,1,0:T(8,128)(2,1)S(1)}, u32[]{:S(2)}, u32[]{:S(2)}) collective-permute-start(bf16[1,128,1024]{2,1,0:T(8,128)(2,1)S(1)} %add_convert_fusion.13), channel_id=1, source_target_pairs={{0,16},{2,18},{4,20},{6,22},{8,24},{10,26},{12,28},{14,30},{16,0},... | collective-permute-start | bytes 786440 | tf_op jit(solution)/shard_map/ppermute | solution.py:12
  539.5 1.4 collective-permute-start.29
  (49 other events, 310.3 us)
